TPU v7x, 32 devices: a whole 2x2x4 slice. The times are simulated.
32 devices in a mesh: batch: 8 (over y, x, core), lib: 4 (over z).
Axes of the slice: x: 2, y: 2, z: 4, core: 2. Of those that a mesh axis runs over, the one named last changes fastest.
Arguments:
- skip_features: bfloat16 [64, 1024, 320], P(('batch', 'lib')), may hold values from -6 to 6
- cached_deep_features: bfloat16 [64, 1024, 640], P('lib', 'batch'), may hold values from -6 to 6
- target_position: int32 [4, 16], P('lib'), may hold values from 0 to 15, each once within a row
- request_adapter: int32 [64], P(('batch', 'lib')), may hold values from 0 to 15
- library_adapter: int32 [16], P('lib'), may hold values from 0 to 15, each once
- adapter_down_weight: bfloat16 [16, 64, 960], P('lib'), may hold values from -0.1875 to 0.1875
- adapter_up_weight: bfloat16 [16, 64, 320], P('lib'), may hold values from -0.75 to 0.75
- kernel_weight: bfloat16 [3, 3, 960, 320], replicated, may hold values from -0.0625 to 0.0625
- shortcut_matrix: bfloat16 [960, 320], replicated, may hold values from -0.1875 to 0.1875
- group_norm_gain: float32 [960], replicated, may hold values from 0.5 to 1.5
- group_norm_offset: float32 [960], replicated, may hold values from -1.8 to 1.8
- output_bias: float32 [320], replicated, may hold values from -1.8 to 1.8
Outputs:
- block_out: bfloat16 [64, 1024, 320], P(('batch', 'lib'))
Inputs may be any that keep to these rules, and one draw needn't show every extreme that they name: Each row of target_position names every one of its 16 slots once. `request_adapter`: ids of adapters in the library. `library_adapter`: every adapter id is held in exactly one library slot.
All inputs are finite; a program needn't handle non-finite values.
Results may differ from a plain program's by a relative error of at most 0.0045.
Values may be sent and summed in bfloat16 or wider, within the bound.
A program may use at most 128 MiB of HBM per device.

v0:
```python
import jax
import jax.numpy as jnp
from jax import lax
from jax.sharding import PartitionSpec as P

DEEP = 640
GROUPS = 32
ROWS = 32
LAT_W = 32


def norm_silu(joined, group_norm_gain, group_norm_offset):
    count = joined.shape[0]
    places = joined.shape[1]
    width = joined.shape[2]
    values = joined.astype(jnp.float32).reshape(count, places, GROUPS, width // GROUPS)
    center = jnp.mean(values, axis=(1, 3), keepdims=True)
    spread = jnp.mean((values - center) ** 2, axis=(1, 3), keepdims=True)
    scaled = ((values - center) / jnp.sqrt(spread + 1e-05)).reshape(
        count, places, width
    ) * group_norm_gain + group_norm_offset
    return jax.nn.silu(scaled).astype(jnp.bfloat16)


def local(
    skip_features,
    cached_deep_features,
    target_position,
    request_adapter,
    library_adapter,
    adapter_down_weight,
    adapter_up_weight,
    kernel_weight,
    shortcut_matrix,
    group_norm_gain,
    group_norm_offset,
    output_bias,
):
    batch_count = lax.axis_size("batch")
    per_device = skip_features.shape[0]
    places = skip_features.shape[1]
    column = target_position.shape[1]
    width = kernel_weight.shape[2]
    outputs = kernel_weight.shape[3]
    placing = target_position[0]
    inverse = jnp.zeros((column,), jnp.int32).at[placing].set(jnp.arange(column, dtype=jnp.int32))
    order = inverse.reshape(batch_count, per_device).T
    outgoing = cached_deep_features[order]
    arrived = lax.all_to_all(outgoing, "batch", split_axis=1, concat_axis=1, tiled=True)
    deep = arrived.reshape(per_device, places, DEEP)
    down_portion = lax.all_gather(adapter_down_weight, "lib", axis=0, tiled=True)
    up_portion = lax.all_gather(adapter_up_weight, "lib", axis=0, tiled=True)
    id_piece = lax.all_gather(library_adapter, "lib", axis=0, tiled=True)
    picker = (request_adapter[:, None] == id_piece[None, :]).astype(jnp.bfloat16)
    down_sum = jnp.einsum("rk,kij->rij", picker, down_portion, preferred_element_type=jnp.float32)
    up_sum = jnp.einsum("rk,kij->rij", picker, up_portion, preferred_element_type=jnp.float32)
    down_sum, up_sum = (down_sum, up_sum)
    down_blocks = down_sum.astype(jnp.bfloat16)
    up_blocks = up_sum.astype(jnp.bfloat16)
    joined = jnp.concatenate([skip_features, deep], axis=2)
    normed = norm_silu(joined, group_norm_gain, group_norm_offset)
    padded = jnp.pad(
        normed.reshape(per_device, ROWS, LAT_W, width), ((0, 0), (1, 1), (1, 1), (0, 0))
    )
    conv = jnp.zeros((per_device * places, outputs), jnp.float32)
    for row_off in range(3):
        for col_off in range(3):
            window = padded[:, row_off : row_off + ROWS, col_off : col_off + LAT_W].reshape(
                per_device * places, width
            )
            conv = conv + jnp.dot(
                window, kernel_weight[row_off, col_off], preferred_element_type=jnp.float32
            )
    shortcut = jnp.dot(
        joined.reshape(per_device * places, width),
        shortcut_matrix,
        preferred_element_type=jnp.float32,
    )
    low = jnp.einsum(
        "rpc,rkc->rpk", normed, down_blocks, preferred_element_type=jnp.float32
    ).astype(jnp.bfloat16)
    delta = jnp.einsum("rpk,rko->rpo", low, up_blocks, preferred_element_type=jnp.float32)
    total = (shortcut + conv).reshape(per_device, places, outputs) + output_bias + delta
    return total.astype(jnp.bfloat16)


def solution(mesh):
    in_specs = (
        P(("batch", "lib"), None, None),
        P("lib", "batch", None),
        P("lib", None),
        P(("batch", "lib")),
        P("lib"),
        P("lib", None, None),
        P("lib", None, None),
        P(),
        P(),
        P(),
        P(),
        P(),
    )
    out_specs = P(("batch", "lib"), None, None)
    return jax.shard_map(local, mesh=mesh, in_specs=in_specs, out_specs=out_specs, check_vma=False)
```

profile of v0, /device:TPU:0, one launch (start us, length us, event | category | flops | bytes accessed | tf_op | source)
XLA Modules:
  0.0 148.1 jit_solution(5434966734072437644)
XLA Ops:
  8.3 2.4 %gather_fusion = bf16[16,128,640]{2,1,0:T(8,128)(2,1)} fusion(bf16[16,128,640]{2,1,0:T(8,128)(2,1)S(1)} %copy-done, s32[1024]{0:T(1024)S(1)} %pad_clamp_fusion), kind=kCustom, calls=%fused_computation | custom fusion | bytes 5242944 | tf_op jit(solution)/shard_map/gather | solution.py:48
  10.7 3.6 %copy.34 = bf16[2,8,128,640]{3,2,0,1:T(8,128)(2,1)} copy(bf16[2,8,128,640]{3,2,1,0:T(8,128)(2,1)} %bitcast.86) | data formatting | bytes 5242880 | tf_op jit(solution)/shard_map/gather | solution.py:48
  14.3 5.3 %all-to-all-start = ((bf16[2,8,128,640]{3,2,0,1:T(8,128)(2,1)}), bf16[2,8,128,640]{3,2,0,1:T(8,128)(2,1)}, u32[]{:S(2)}, u32[]{:S(2)}) async-start(bf16[2,8,128,640]{3,2,0,1:T(8,128)(2,1)} %copy.34), calls=%async_computation | async-start | bytes 5242880 | tf_op jit(solution)/shard_map/all_to_all | solution.py:49
  20.3 1.6 %copy.49 = bf16[2,1024,320]{2,1,0:T(8,128)(2,1)} copy(bf16[2,1024,320]{1,2,0:T(8,128)(2,1)S(1)} %copy-done.9) | data formatting | bytes 2621440 | tf_op jit(solution)/shard_map/concatenate | solution.py:60
  23.4 9.2 %all-reduce.1 = s32[16]{0:T(128)S(1)} all-reduce(s32[16]{0:T(128)S(1)} %dynamic-update-slice), channel_id=1, replica_groups=mesh['batch'=8,'lib'=4] {'lib'}, use_global_device_ids=true, to_apply=%add.1 | all-reduce | flops 16 | bytes 128
  32.6 29.5 %all_gather.11 = bf16[16,64,320]{2,1,0:T(8,128)(2,1)S(1)} all-gather(bf16[4,64,320]{2,1,0:T(8,128)(2,1)S(1)} %copy-done.10), channel_id=1, replica_groups=mesh['batch'=8,'lib'=4] {'lib'}, dimensions={0}, use_global_device_ids=true | all-gather | bytes 819200 | tf_op jit(solution)/shard_map/all_gather | solution.py:52
  62.7 2.2 %copy.35 = bf16[2,8,128,640]{3,2,1,0:T(8,128)(2,1)S(1)} copy(bf16[2,8,128,640]{3,2,0,1:T(8,128)(2,1)} %all-to-all-done) | data formatting | bytes 5242880 | tf_op jit(solution)/shard_map/all_to_all | solution.py:49
  64.9 1.7 %convert_reduce_fusion = f32[2,960]{1,0:T(2,128)S(1)} fusion(bf16[2,1024,640]{2,1,0:T(8,128)(2,1)S(1)} %bitcast.72, bf16[2,1024,320]{2,1,0:T(8,128)(2,1)S(1)} %copy-done.2), kind=kLoop, calls=%fused_computation.3 | loop fusion | flops 9828480 | bytes 3939840 | tf_op jit(solution)/shard_map/reduce_sum | solution.py:17
  67.1 3.6 %fusion.2 = f32[2,960]{1,0:T(2,128)S(1)} fusion(f32[2,960]{1,0:T(2,128)S(1)} %sub.32, bf16[2,1024,640]{2,1,0:T(8,128)(2,1)S(1)} %bitcast.73, bf16[2,1024,320]{2,1,0:T(8,128)(2,1)} %copy.49), kind=kLoop, calls=%fused_computation.6 | loop fusion | flops 13760640 | bytes 3947520 | tf_op jit(solution)/shard_map/reduce_sum | solution.py:18
  71.1 6.8 %multiply_convert_fusion = bf16[2,1024,960]{2,1,0:T(8,128)(2,1)} fusion(f32[960]{0:T(1024)S(1)} %copy-done.11, f32[960]{0:T(1024)S(1)} %copy-done.12, f32[2,960]{1,0:T(2,128)S(1)} %div.50, f32[2,960]{1,0:T(2,128)S(1)} %sub.32, bf16[2,1024,640]{2,1,0:T(8,128)(2,1)S(1)} %bitcast.74, bf16[2,1024,320]{2,1,0:T(8,128)(2,1)} %copy.49), kind=kLoop, calls=%fused_computation.9 | loop fusion | flops 25559040 | bytes 7887360 | tf_op jit(solution)/shard_map/convert_element_type | solution.py:22
  77.9 5.6 %multiply_convert_fusion.1 = bf16[2,32,32,960]{3,2,1,0:T(8,128)(2,1)} fusion(bf16[2,32,32,640]{3,2,1,0:T(8,128)(2,1)S(1)} %bitcast.75, bf16[2,32,32,320]{3,2,1,0:T(8,128)(2,1)S(1)} %bitcast.77, f32[960]{0:T(1024)S(1)} %copy-done.11, f32[960]{0:T(1024)S(1)} %copy-done.12, f32[2,960]{1,0:T(2,128)S(1)} %div.50, f32[2,960]{1,0:T(2,128)S(1)} %sub.32), kind=kLoop, calls=%fused_computation.10 | loop fusion | flops 25559040 | bytes 7887360 | tf_op jit(solution)/shard_map/convert_element_type | solution.py:22
  83.5 22.2 %pad_slice_fusion = (bf16[2,32,32,960]{3,2,1,0:T(8,128)(2,1)S(1)}, bf16[2,32,32,960]{3,2,1,0:T(8,128)(2,1)}, bf16[2,32,32,960]{3,2,1,0:T(8,128)(2,1)}, bf16[2,32...) fusion(bf16[2,32,32,960]{3,2,1,0:T(8,128)(2,1)} %multiply_conve, ...), kind=kLoop, calls=%fused_computation.11 | loop fusion | bytes 35389440 | tf_op jit(solution)/shard_map/slice | solution.py:68
  105.8 4.1 %fusion.30 = f32[2048,320]{0,1:T(8,128)S(1)} fusion(bf16[2048,960]{1,0:T(8,128)(2,1)} %bitcast.88, bf16[3,3,960,320]{2,3,1,0:T(8,128)(2,1)} %param.19), kind=kOutput, calls=%fused_computation.51 | convolution fusion | flops 1258291200 | bytes 7471104 | tf_op jit(solution)/shard_map/dot_general | solution.py:71
  109.9 2.8 %convolution_add_fusion.6 = f32[2048,320]{0,1:T(8,128)S(1)} fusion(f32[2048,320]{0,1:T(8,128)S(1)} %fusion.30, bf16[2048,960]{1,0:T(8,128)(2,1)S(1)} %bitcast.84, bf16[3,3,960,320]{2,3,1,0:T(8,128)(2,1)} %param.19), kind=kOutput, calls=%fused_computation.32 | convolution fusion | flops 1258946560 | bytes 9830400 | tf_op jit(solution)/shard_map/dot_general | solution.py:71
  112.9 1.6 %convolution_add_fusion.5 = f32[2048,320]{0,1:T(8,128)S(1)} fusion(f32[2048,320]{0,1:T(8,128)S(1)} %convolution_add_fusion.6, bf16[2048,960]{1,0:T(8,128)(2,1)S(1)} %bitcast.83, bf16[3,3,960,320]{2,3,1,0:T(8,128)(2,1)S(1)} %bitcast.90), kind=kOutput, calls=%fused_computation.31 | convolution fusion | flops 1258946560 | bytes 10092544 | tf_op jit(solution)/shard_map/dot_general | solution.py:71
  115.1 1.6 %convolution_add_fusion.4 = f32[2048,320]{0,1:T(8,128)S(1)} fusion(f32[2048,320]{0,1:T(8,128)S(1)} %convolution_add_fusion.5, bf16[2048,960]{1,0:T(8,128)(2,1)S(1)} %bitcast.82, bf16[3,3,960,320]{2,3,1,0:T(8,128)(2,1)S(1)} %bitcast.90), kind=kOutput, calls=%fused_computation.30 | convolution fusion | flops 1258946560 | bytes 10092544 | tf_op jit(solution)/shard_map/dot_general | solution.py:71
  117.3 3.1 %fusion.24 = f32[2048,320]{0,1:T(8,128)} fusion(bf16[2048,960]{1,0:T(8,128)(2,1)S(1)} %bitcast.87, bf16[3,3,960,320]{2,3,1,0:T(8,128)(2,1)S(1)} %bitcast.90), kind=kOutput, calls=%fused_computation.45 | convolution fusion | flops 1258291200 | bytes 7471104 | tf_op jit(solution)/shard_map/dot_general | solution.py:71
  120.4 3.5 %fusion.12 = f32[2048,320]{0,1:T(8,128)S(1)} fusion(f32[2048,320]{0,1:T(8,128)} %fusion.24, f32[2048,320]{0,1:T(8,128)S(1)} %convolution_add_fusion.4, bf16[2048,960]{1,0:T(8,128)(2,1)S(1)} %bitcast.85, bf16[3,3,960,320]{2,3,1,0:T(8,128)(2,1)S(1)} %bitcast.90), kind=kOutput, calls=%fused_computation.26 | convolution fusion | flops 1259601920 | bytes 12713984 | tf_op jit(solution)/shard_map/dot_general | solution.py:71
  123.9 1.6 %convolution_add_fusion.3 = f32[2048,320]{0,1:T(8,128)S(1)} fusion(f32[2048,320]{0,1:T(8,128)S(1)} %fusion.12, bf16[2048,960]{1,0:T(8,128)(2,1)S(1)} %bitcast.81, bf16[3,3,960,320]{2,3,1,0:T(8,128)(2,1)S(1)} %bitcast.90), kind=kOutput, calls=%fused_computation.29 | convolution fusion | flops 1258946560 | bytes 10092544 | tf_op jit(solution)/shard_map/dot_general | solution.py:71
  125.5 1.6 %convolution_add_fusion.2 = f32[2048,320]{0,1:T(8,128)S(1)} fusion(f32[2048,320]{0,1:T(8,128)S(1)} %convolution_add_fusion.3, bf16[2048,960]{1,0:T(8,128)(2,1)S(1)} %bitcast.80, bf16[3,3,960,320]{2,3,1,0:T(8,128)(2,1)S(1)} %bitcast.90), kind=kOutput, calls=%fused_computation.28 | convolution fusion | flops 1258946560 | bytes 10092544 | tf_op jit(solution)/shard_map/dot_general | solution.py:71
  127.2 1.9 %convolution_add_fusion.1 = f32[2048,320]{0,1:T(8,128)S(1)} fusion(f32[2048,320]{0,1:T(8,128)S(1)} %convolution_add_fusion.2, bf16[2048,960]{1,0:T(8,128)(2,1)S(1)} %bitcast.79, bf16[3,3,960,320]{2,3,1,0:T(8,128)(2,1)S(1)} %bitcast.90), kind=kOutput, calls=%fused_computation.27 | convolution fusion | flops 1258946560 | bytes 10092544 | tf_op jit(solution)/shard_map/dot_general | solution.py:71
  129.1 3.3 %fusion.9 = f32[2048,320]{0,1:T(8,128)} fusion(f32[2048,320]{0,1:T(8,128)S(1)} %convolution_add_fusion.1, bf16[960,320]{0,1:T(8,128)(2,1)S(1)} %copy-done.15, bf16[2048,640]{1,0:T(8,128)(2,1)S(1)} %bitcast.76, bf16[2048,320]{1,0:T(8,128)(2,1)S(1)} %bitcast.78), kind=kOutput, calls=%fused_computation.24 | convolution fusion | flops 1266810880 | bytes 9789440 | tf_op jit(solution)/shard_map/dot_general | solution.py:74
  132.4 2.9 %fusion.17 = bf16[2,64,960]{2,0,1:T(2,128)(2,1)S(1)} fusion(bf16[16,64,960]{2,1,0:T(8,128)(2,1)} %all-gather.2.cloned.1.call-done, s32[16]{0:T(128)S(1)} %all-reduce.1, s32[2]{0:T(128)S(1)} %copy-done.14), kind=kOutput, calls=%fused_computation.39 | convolution fusion | flops 4055072 | bytes 2211912 | tf_op jit(solution)/shard_map/rk,kij->rij/dot_general | solution.py:55
  135.3 6.0 %fusion.14 = bf16[2,1024,320]{1,2,0:T(8,128)(2,1)} fusion(f32[40,2,8,1024]{3,2,1,0:T(8,128)} %bitcast.91, f32[320]{0:T(512)S(1)} %copy-done.13, bf16[2,1024,960]{2,1,0:T(8,128)(2,1)} %multiply_convert_fusion, bf16[2,64,960]{2,0,1:T(2,128)(2,1)S(1)} %fusion.17, bf16[2,64,320]{2,0,1:T(2,128)(2,1)S(1)} %convolution_convert_fusion.1), kind=kOutput, calls=%fused_computation.35 | convolution fusion | flops 337641472 | bytes 8193280 | tf_op jit(solution)/shard_map/rpk,rko->rpo/dot_general | solution.py:82
  (67 shorter events, 6.1 us)
Async XLA Ops:
  6.5 1.8 %copy-start = (bf16[16,128,640]{2,1,0:T(8,128)(2,1)S(1)}, bf16[16,128,640]{2,1,0:T(8,128)(2,1)}, u32[]{:S(2)}) copy-start(bf16[16,128,640]{2,1,0:T(8,128)(2,1)} %param.13) | copy-start | bytes 7864324
  14.3 6.1 %copy-start.9 = (bf16[2,1024,320]{1,2,0:T(8,128)(2,1)S(1)}, bf16[2,1024,320]{1,2,0:T(8,128)(2,1)}, u32[]{:S(2)}) copy-start(bf16[2,1024,320]{1,2,0:T(8,128)(2,1)} %param.12) | copy-start | bytes 3932164
  14.3 7.7 %copy-start.17 = (u32[32]{0:T(128)S(1)}, u32[32]{0:T(128)}, u32[]{:S(2)}) copy-start(u32[32]{0:T(128)} %constant.27) | copy-start | bytes 388
  14.3 8.9 %copy-start.16 = (s32[4]{0:T(128)S(1)}, s32[4]{0:T(128)}, u32[]{:S(2)}) copy-start(s32[4]{0:T(128)} %param.16) | copy-start | bytes 52
  14.3 18.3 %copy-start.10 = (bf16[4,64,320]{2,1,0:T(8,128)(2,1)S(1)}, bf16[4,64,320]{2,1,0:T(8,128)(2,1)}, u32[]{:S(2)}) copy-start(bf16[4,64,320]{2,1,0:T(8,128)(2,1)} %param.18) | copy-start | bytes 491524
  14.3 47.8 %copy-start.14 = (s32[2]{0:T(128)S(1)}, s32[2]{0:T(128)}, u32[]{:S(2)}) copy-start(s32[2]{0:T(128)} %param.15) | copy-start | bytes 28
  14.3 48.4 %all-to-all-start = ((bf16[2,8,128,640]{3,2,0,1:T(8,128)(2,1)}), bf16[2,8,128,640]{3,2,0,1:T(8,128)(2,1)}, u32[]{:S(2)}, u32[]{:S(2)}) async-start(bf16[2,8,128,640]{3,2,0,1:T(8,128)(2,1)} %copy.34), calls=%async_computation | async-start | bytes 5242880 | tf_op jit(solution)/shard_map/all_to_all | solution.py:49
  19.6 112.8 %all-gather.2.cloned.1.call-start = ((), (), s32[]{:S(2)}) async-start(), calls=%async_computation.1 | async-start | bytes 2621440 | tf_op jit(solution)/shard_map/all_gather | solution.py:51
  62.7 2.2 %copy-start.2 = (bf16[2,1024,320]{2,1,0:T(8,128)(2,1)S(1)}, bf16[2,1024,320]{2,1,0:T(8,128)(2,1)}, u32[]{:S(2)}) copy-start(bf16[2,1024,320]{2,1,0:T(8,128)(2,1)} %copy.49) | copy-start | bytes 3932164
  64.9 6.2 %copy-start.11 = (f32[960]{0:T(1024)S(1)}, f32[960]{0:T(1024)}, u32[]{:S(2)}) copy-start(f32[960]{0:T(1024)} %param.22) | copy-start | bytes 11524
  64.9 6.2 %copy-start.12 = (f32[960]{0:T(1024)S(1)}, f32[960]{0:T(1024)}, u32[]{:S(2)}) copy-start(f32[960]{0:T(1024)} %param.21) | copy-start | bytes 11524
  71.1 6.9 %copy-start.3 = (bf16[2,1024,320]{2,1,0:T(8,128)(2,1)S(1)}, bf16[2,1024,320]{2,1,0:T(8,128)(2,1)}, u32[]{:S(2)}) copy-start(bf16[2,1024,320]{2,1,0:T(8,128)(2,1)} %copy.49) | copy-start | bytes 3932164
  105.8 4.1 %copy-start.6 = (bf16[2,32,32,960]{3,2,1,0:T(8,128)(2,1)S(1)}, bf16[2,32,32,960]{3,2,1,0:T(8,128)(2,1)}, u32[]{:S(2)}) copy-start(bf16[2,32,32,960]{3,2,1,0:T(8,128)(2,1)} %get-tuple-element.6) | copy-start | bytes 11796484
  105.8 6.9 %slice-start = ((s8[5898240]{0:T(1024)(128)(4,1)}), s8[4194304]{0:T(1024)(128)(4,1)S(1)}, s32[]{:S(2)}) async-start(s8[5898240]{0:T(1024)(128)(4,1)} %bitcast.89), calls=%async_computation.2 | async-start | bytes 8388608
  109.9 2.9 %copy-start.5 = (bf16[2,32,32,960]{3,2,1,0:T(8,128)(2,1)S(1)}, bf16[2,32,32,960]{3,2,1,0:T(8,128)(2,1)}, u32[]{:S(2)}) copy-start(bf16[2,32,32,960]{3,2,1,0:T(8,128)(2,1)} %get-tuple-element.7) | copy-start | bytes 11796484
  109.9 3.0 %slice-start.1 = ((s8[5898240]{0:T(1024)(128)(4,1)}), s8[1703936]{0:T(1024)(128)(4,1)S(1)}, s32[]{:S(2)}) async-start(s8[5898240]{0:T(1024)(128)(4,1)} %bitcast.89), calls=%async_computation.3 | async-start | bytes 3407872
  112.9 2.2 %copy-start.4 = (bf16[2,32,32,960]{3,2,1,0:T(8,128)(2,1)S(1)}, bf16[2,32,32,960]{3,2,1,0:T(8,128)(2,1)}, u32[]{:S(2)}) copy-start(bf16[2,32,32,960]{3,2,1,0:T(8,128)(2,1)} %get-tuple-element.8) | copy-start | bytes 11796484
  115.1 2.2 %copy-start.8 = (bf16[2,32,32,960]{3,2,1,0:T(8,128)(2,1)S(1)}, bf16[2,32,32,960]{3,2,1,0:T(8,128)(2,1)}, u32[]{:S(2)}) copy-start(bf16[2,32,32,960]{3,2,1,0:T(8,128)(2,1)} %get-tuple-element.9) | copy-start | bytes 11796484
  117.3 3.1 %copy-start.7 = (bf16[2,1024,960]{2,1,0:T(8,128)(2,1)S(1)}, bf16[2,1024,960]{2,1,0:T(8,128)(2,1)}, u32[]{:S(2)}) copy-start(bf16[2,1024,960]{2,1,0:T(8,128)(2,1)} %multiply_convert_fusion) | copy-start | bytes 11796484
  127.2 1.9 %copy-start.15 = (bf16[960,320]{0,1:T(8,128)(2,1)S(1)}, bf16[960,320]{0,1:T(8,128)(2,1)}, u32[]{:S(2)}) copy-start(bf16[960,320]{0,1:T(8,128)(2,1)} %param.20) | copy-start | bytes 1843204
  129.1 6.2 %copy-start.13 = (f32[320]{0:T(512)S(1)}, f32[320]{0:T(512)}, u32[]{:S(2)}) copy-start(f32[320]{0:T(512)} %param.23) | copy-start | bytes 3844
  135.3 6.0 %copy-start.1 = (bf16[16,128,640]{2,1,0:T(8,128)(2,1)S(1)}, bf16[16,128,640]{2,1,0:T(8,128)(2,1)}, u32[]{:S(2)}) copy-start(bf16[16,128,640]{2,1,0:T(8,128)(2,1)} %param.13) | copy-start | bytes 7864324
Sparse Core Ops, SparseCore 0:
  22.0 60.5 all-gather.1
where the time goes:
time: 149 us; the launch traced here: 148 us
  blocking collectives  38.7 us (26%)
  local copies, waits for them, and re-layouts  35.9 us (24%)
  matrix products  34.4 us (23%)
  other arithmetic  18.8 us (13%)
  between operations  14.4 us (10%)
  starting transfers between devices  5.35 us (4%)
    all_gather x1, blocking collectives, local(): up_portion = lax.all_gather(adapter_up_weight, 'lib', axis=0, tiled=True)  29.5 us
    slice x1, local copies, waits for them, and re-layouts, local(): padded[:, row_off:row_off + ROWS, col_off:col_off + LAT_W]  22.2 us
    dot_general x9, matrix products, local(): jnp.dot(window, kernel_weight[row_off, col_off], preferred_element_type=j...  21.7 us
    convert_element_type x2, other arithmetic, norm_silu(): return jax.nn.silu(scaled).astype(jnp.bfloat16)  12.4 us
    unnamed x1, blocking collectives  9.15 us
    dot_general x1, matrix products, local(): jnp.einsum('rpk,rko->rpo', low, up_blocks, preferred_element_type=jnp.flo...  5.97 us
    gather x2, local copies, waits for them, and re-layouts, local(): outgoing = cached_deep_features[order]  5.97 us
    all_to_all x1, starting transfers between devices, local(): lax.all_to_all(outgoing, 'batch', split_axis=1, concat_axis=1, tiled=True)  5.31 us
  transfers between devices with their start and end apart: 2, of which 0 were waited for; matrix products, arithmetic and copies ran while one was open for 48% of the time, Pallas kernels for 0%

commit v1 on v0

--- a/solution.py
+++ b/solution.py
@@ -49,7 +49,12 @@
     arrived = lax.all_to_all(outgoing, "batch", split_axis=1, concat_axis=1, tiled=True)
     deep = arrived.reshape(per_device, places, DEEP)
     down_portion = lax.all_gather(adapter_down_weight, "lib", axis=0, tiled=True)
-    up_portion = lax.all_gather(adapter_up_weight, "lib", axis=0, tiled=True)
+    ring = [adapter_up_weight]
+    for hop in range(3):
+        ring.append(lax.ppermute(ring[-1], "lib", [(dev, (dev + 1) % 4) for dev in range(4)]))
+    up_portion = jnp.roll(
+        jnp.concatenate(ring[::-1], axis=0), (lax.axis_index("lib") + 1) * ring[0].shape[0], axis=0
+    )
     id_piece = lax.all_gather(library_adapter, "lib", axis=0, tiled=True)
     picker = (request_adapter[:, None] == id_piece[None, :]).astype(jnp.bfloat16)
     down_sum = jnp.einsum("rk,kij->rij", picker, down_portion, preferred_element_type=jnp.float32)

time: 149 us -> 140 us (0.940)
  blocking collectives: 38.7 us -> 8.23 us
  waiting for transfers between devices: 0.68 us -> 16.1 us
  starting transfers between devices: 5.35 us -> 7.68 us
  local copies, waits for them, and re-layouts: 35.9 us -> 38.2 us
  other arithmetic: 18.8 us -> 20.5 us
    all_gather x1 -> x0, blocking collectives: 29.5 us -> none  [local(): up_portion = lax.all_gather(adapter_up_weight, 'lib', axis=0, tiled=True)]
    ppermute x0 -> x3, waiting for transfers between devices: none -> 15.8 us  [local(): lax.ppermute(ring[-1], 'lib', [(dev, (dev + 1) % 4) for dev in range(4)])]
    ppermute x0 -> x3, starting transfers between devices: none -> 2.34 us  [local(): lax.ppermute(ring[-1], 'lib', [(dev, (dev + 1) % 4) for dev in range(4)])]
    concatenate x0 -> x1, local copies, waits for them, and re-layouts: none -> 1.96 us  [local(): jnp.roll(jnp.concatenate(ring[::-1], axis=0), (lax.axis_index('lib') + 1)...]
    reduce_sum x2, other arithmetic: 1.82 us -> 3.5 us  [norm_silu(): center = jnp.mean(values, axis=(1, 3), keepdims=True)]
  transfers between devices with their start and end apart: 2 -> 5, of which waited for: 0 -> 3; matrix products, arithmetic and copies ran while one was open for 48% -> 54% of each run, Pallas kernels for 0% -> 0%
where the time goes in v1:
time: 140 us; the launch traced here: 139 us
  local copies, waits for them, and re-layouts  38.2 us (27%)
  matrix products  34.2 us (24%)
  other arithmetic  20.5 us (15%)
  waiting for transfers between devices  16.1 us (12%)
  between operations  14.4 us (10%)
  blocking collectives  8.23 us (6%)
  starting transfers between devices  7.68 us (5%)
    slice x1, local copies, waits for them, and re-layouts, local(): padded[:, row_off:row_off + ROWS, col_off:col_off + LAT_W]  22.5 us
    dot_general x9, matrix products, local(): jnp.dot(window, kernel_weight[row_off, col_off], preferred_element_type=j...  21.7 us
    ppermute x3, waiting for transfers between devices, local(): lax.ppermute(ring[-1], 'lib', [(dev, (dev + 1) % 4) for dev in range(4)])  15.8 us
    convert_element_type x2, other arithmetic, norm_silu(): return jax.nn.silu(scaled).astype(jnp.bfloat16)  12.4 us
    unnamed x1, blocking collectives  8.23 us
    gather x2, local copies, waits for them, and re-layouts, local(): outgoing = cached_deep_features[order]  6.01 us
    dot_general x1, matrix products, local(): jnp.einsum('rpk,rko->rpo', low, up_blocks, preferred_element_type=jnp.flo...  5.96 us
    all_to_all x1, starting transfers between devices, local(): lax.all_to_all(outgoing, 'batch', split_axis=1, concat_axis=1, tiled=True)  5.3 us
  transfers between devices with their start and end apart: 5, of which 3 were waited for; matrix products, arithmetic and copies ran while one was open for 54% of the time, Pallas kernels for 0%

profile of v1, /device:TPU:0, one launch (start us, length us, event | category | flops | bytes accessed | tf_op | source)
XLA Modules:
  0.0 139.2 jit_solution(11728696801594866323)
XLA Ops:
  8.3 2.4 %gather_fusion = bf16[16,128,640]{2,1,0:T(8,128)(2,1)} fusion(bf16[16,128,640]{2,1,0:T(8,128)(2,1)S(1)} %copy-done, s32[1024]{0:T(1024)S(1)} %pad_clamp_fusion), kind=kCustom, calls=%fused_computation | custom fusion | bytes 5242944 | tf_op jit(solution)/shard_map/gather | solution.py:48
  10.7 3.6 %copy.36 = bf16[2,8,128,640]{3,2,0,1:T(8,128)(2,1)} copy(bf16[2,8,128,640]{3,2,1,0:T(8,128)(2,1)} %bitcast.86) | data formatting | bytes 5242880 | tf_op jit(solution)/shard_map/gather | solution.py:48
  14.3 5.3 %all-to-all-start = ((bf16[2,8,128,640]{3,2,0,1:T(8,128)(2,1)}), bf16[2,8,128,640]{3,2,0,1:T(8,128)(2,1)}, u32[]{:S(2)}, u32[]{:S(2)}) async-start(bf16[2,8,128,640]{3,2,0,1:T(8,128)(2,1)} %copy.36), calls=%async_computation | async-start | bytes 5242880 | tf_op jit(solution)/shard_map/all_to_all | solution.py:49
  19.8 2.3 %collective-permute-start = (bf16[4,64,320]{2,0,1:T(4,128)(2,1)S(1)}, bf16[4,64,320]{2,0,1:T(4,128)(2,1)S(1)}, u32[]{:S(2)}, u32[]{:S(2)}) collective-permute-start(bf16[4,64,320]{2,0,1:T(4,128)(2,1)S(1)} %copy.48), channel_id=1, source_target_pairs={{0,1},{1,2},{2,3},{3,0},{4,5},{5,6},{6,7},{7,4},{8,9},{9,10},{10,1... | collective-permute-start | bytes 491528 | tf_op jit(solution)/shard_map/ppermute | solution.py:54
  22.2 7.4 %collective-permute-done = bf16[4,64,320]{2,0,1:T(4,128)(2,1)S(1)} collective-permute-done((bf16[4,64,320]{2,0,1:T(4,128)(2,1)S(1)}, bf16[4,64,320]{2,0,1:T(4,128)(2,1)S(1)}, u32[]{:S(2)}, u32[]{:S(2)}) %collective-permute-start) | collective-permute-done | bytes 163872 | tf_op jit(solution)/shard_map/ppermute | solution.py:54
  29.6 8.4 %collective-permute-done.1 = bf16[4,64,320]{2,0,1:T(4,128)(2,1)S(1)} collective-permute-done((bf16[4,64,320]{2,0,1:T(4,128)(2,1)S(1)}, bf16[4,64,320]{2,0,1:T(4,128)(2,1)S(1)}, u32[]{:S(2)}, u32[]{:S(2)}) %collective-permute-start.1) | collective-permute-done | bytes 163872 | tf_op jit(solution)/shard_map/ppermute | solution.py:54
  41.2 8.2 %all-reduce.1 = s32[16]{0:T(128)S(1)} all-reduce(s32[16]{0:T(128)S(1)} %dynamic-update-slice), channel_id=1, replica_groups=mesh['batch'=8,'lib'=4] {'lib'}, use_global_device_ids=true, to_apply=%add.1 | all-reduce | flops 16 | bytes 128
  49.4 2.0 %concatenate.38 = bf16[32,64,320]{2,0,1:T(8,128)(2,1)S(1)} concatenate(bf16[4,64,320]{2,0,1:T(4,128)(2,1)S(1)} %collective-permute-done.2, bf16[4,64,320]{2,0,1:T(4,128)(2,1)S(1)} %collective-permute-done.1, bf16[4,64,320]{2,0,1:T(4,128)(2,1)S(1)} %collective-permute-done, bf16[4,64,320]{2,0,1:T(4,128)(2,1)S(1)} %copy.48, bf16[4,64,320]{2,0,1:T(4,128)(2,1)S(1)} %collective-permute-done.2, ...), dimensions={0} | concatenate | bytes 2621440 | tf_op jit(solution)/shard_map/jit(_roll_dynamic)/concatenate | solution.py:55
  52.0 2.1 %copy.37 = bf16[2,8,128,640]{3,2,1,0:T(8,128)(2,1)S(1)} copy(bf16[2,8,128,640]{3,2,0,1:T(8,128)(2,1)} %all-to-all-done) | data formatting | bytes 5242880 | tf_op jit(solution)/shard_map/all_to_all | solution.py:49
  54.1 3.4 %convert_reduce_fusion = f32[2,960]{1,0:T(2,128)S(1)} fusion(bf16[2,1024,640]{2,1,0:T(8,128)(2,1)S(1)} %bitcast.72, bf16[2,1024,320]{2,1,0:T(8,128)(2,1)} %copy.53), kind=kLoop, calls=%fused_computation.3 | loop fusion | flops 9828480 | bytes 3939840 | tf_op jit(solution)/shard_map/reduce_sum | solution.py:17
  57.9 3.6 %fusion.2 = f32[2,960]{1,0:T(2,128)S(1)} fusion(f32[2,960]{1,0:T(2,128)S(1)} %sub.36, bf16[2,1024,640]{2,1,0:T(8,128)(2,1)S(1)} %bitcast.73, bf16[2,1024,320]{2,1,0:T(8,128)(2,1)} %copy.53), kind=kLoop, calls=%fused_computation.6 | loop fusion | flops 13760640 | bytes 3947520 | tf_op jit(solution)/shard_map/reduce_sum | solution.py:18
  61.9 6.8 %multiply_convert_fusion = bf16[2,1024,960]{2,1,0:T(8,128)(2,1)} fusion(f32[960]{0:T(1024)S(1)} %copy-done.10, f32[960]{0:T(1024)S(1)} %copy-done.11, f32[2,960]{1,0:T(2,128)S(1)} %div.50, f32[2,960]{1,0:T(2,128)S(1)} %sub.36, bf16[2,1024,640]{2,1,0:T(8,128)(2,1)S(1)} %bitcast.74, bf16[2,1024,320]{2,1,0:T(8,128)(2,1)} %copy.53), kind=kLoop, calls=%fused_computation.9 | loop fusion | flops 25559040 | bytes 7887360 | tf_op jit(solution)/shard_map/convert_element_type | solution.py:22
  68.8 5.6 %multiply_convert_fusion.1 = bf16[2,32,32,960]{3,2,1,0:T(8,128)(2,1)} fusion(bf16[2,32,32,640]{3,2,1,0:T(8,128)(2,1)S(1)} %bitcast.75, bf16[2,32,32,320]{3,2,1,0:T(8,128)(2,1)S(1)} %bitcast.77, f32[960]{0:T(1024)S(1)} %copy-done.10, f32[960]{0:T(1024)S(1)} %copy-done.11, f32[2,960]{1,0:T(2,128)S(1)} %div.50, f32[2,960]{1,0:T(2,128)S(1)} %sub.36), kind=kLoop, calls=%fused_computation.10 | loop fusion | flops 25559040 | bytes 7887360 | tf_op jit(solution)/shard_map/convert_element_type | solution.py:22
  74.4 22.5 %pad_slice_fusion = (bf16[2,32,32,960]{3,2,1,0:T(8,128)(2,1)S(1)}, bf16[2,32,32,960]{3,2,1,0:T(8,128)(2,1)}, bf16[2,32,32,960]{3,2,1,0:T(8,128)(2,1)}, bf16[2,32...) fusion(bf16[2,32,32,960]{3,2,1,0:T(8,128)(2,1)} %multiply_conve, ...), kind=kLoop, calls=%fused_computation.11 | loop fusion | bytes 35389440 | tf_op jit(solution)/shard_map/slice | solution.py:73
  96.9 4.0 %fusion.30 = f32[2048,320]{0,1:T(8,128)S(1)} fusion(bf16[2048,960]{1,0:T(8,128)(2,1)} %bitcast.88, bf16[3,3,960,320]{2,3,1,0:T(8,128)(2,1)} %param.19), kind=kOutput, calls=%fused_computation.51 | convolution fusion | flops 1258291200 | bytes 7471104 | tf_op jit(solution)/shard_map/dot_general | solution.py:76
  101.0 2.8 %convolution_add_fusion.6 = f32[2048,320]{0,1:T(8,128)S(1)} fusion(f32[2048,320]{0,1:T(8,128)S(1)} %fusion.30, bf16[2048,960]{1,0:T(8,128)(2,1)S(1)} %bitcast.84, bf16[3,3,960,320]{2,3,1,0:T(8,128)(2,1)} %param.19), kind=kOutput, calls=%fused_computation.32 | convolution fusion | flops 1258946560 | bytes 9830400 | tf_op jit(solution)/shard_map/dot_general | solution.py:76
  108.4 3.1 %fusion.24 = f32[2048,320]{0,1:T(8,128)} fusion(bf16[2048,960]{1,0:T(8,128)(2,1)S(1)} %bitcast.87, bf16[3,3,960,320]{2,3,1,0:T(8,128)(2,1)S(1)} %bitcast.90), kind=kOutput, calls=%fused_computation.45 | convolution fusion | flops 1258291200 | bytes 7471104 | tf_op jit(solution)/shard_map/dot_general | solution.py:76
  111.5 3.5 %fusion.12 = f32[2048,320]{0,1:T(8,128)S(1)} fusion(f32[2048,320]{0,1:T(8,128)} %fusion.24, f32[2048,320]{0,1:T(8,128)S(1)} %convolution_add_fusion.4, bf16[2048,960]{1,0:T(8,128)(2,1)S(1)} %bitcast.85, bf16[3,3,960,320]{2,3,1,0:T(8,128)(2,1)S(1)} %bitcast.90), kind=kOutput, calls=%fused_computation.26 | convolution fusion | flops 1259601920 | bytes 12713984 | tf_op jit(solution)/shard_map/dot_general | solution.py:76
  115.0 1.6 %convolution_add_fusion.3 = f32[2048,320]{0,1:T(8,128)S(1)} fusion(f32[2048,320]{0,1:T(8,128)S(1)} %fusion.12, bf16[2048,960]{1,0:T(8,128)(2,1)S(1)} %bitcast.81, bf16[3,3,960,320]{2,3,1,0:T(8,128)(2,1)S(1)} %bitcast.90), kind=kOutput, calls=%fused_computation.29 | convolution fusion | flops 1258946560 | bytes 10092544 | tf_op jit(solution)/shard_map/dot_general | solution.py:76
  116.6 1.6 %convolution_add_fusion.2 = f32[2048,320]{0,1:T(8,128)S(1)} fusion(f32[2048,320]{0,1:T(8,128)S(1)} %convolution_add_fusion.3, bf16[2048,960]{1,0:T(8,128)(2,1)S(1)} %bitcast.80, bf16[3,3,960,320]{2,3,1,0:T(8,128)(2,1)S(1)} %bitcast.90), kind=kOutput, calls=%fused_computation.28 | convolution fusion | flops 1258946560 | bytes 10092544 | tf_op jit(solution)/shard_map/dot_general | solution.py:76
  118.3 1.9 %convolution_add_fusion.1 = f32[2048,320]{0,1:T(8,128)S(1)} fusion(f32[2048,320]{0,1:T(8,128)S(1)} %convolution_add_fusion.2, bf16[2048,960]{1,0:T(8,128)(2,1)S(1)} %bitcast.79, bf16[3,3,960,320]{2,3,1,0:T(8,128)(2,1)S(1)} %bitcast.90), kind=kOutput, calls=%fused_computation.27 | convolution fusion | flops 1258946560 | bytes 10092544 | tf_op jit(solution)/shard_map/dot_general | solution.py:76
  120.2 3.3 %fusion.9 = f32[2048,320]{0,1:T(8,128)} fusion(f32[2048,320]{0,1:T(8,128)S(1)} %convolution_add_fusion.1, bf16[960,320]{0,1:T(8,128)(2,1)S(1)} %copy-done.14, bf16[2048,640]{1,0:T(8,128)(2,1)S(1)} %bitcast.76, bf16[2048,320]{1,0:T(8,128)(2,1)S(1)} %bitcast.78), kind=kOutput, calls=%fused_computation.24 | convolution fusion | flops 1266810880 | bytes 9789440 | tf_op jit(solution)/shard_map/dot_general | solution.py:79
  123.5 2.9 %fusion.17 = bf16[2,64,960]{2,0,1:T(2,128)(2,1)S(1)} fusion(bf16[16,64,960]{2,1,0:T(8,128)(2,1)} %all-gather.2.cloned.1.call-done, s32[16]{0:T(128)S(1)} %all-reduce.1, s32[2]{0:T(128)S(1)} %copy-done.13), kind=kOutput, calls=%fused_computation.39 | convolution fusion | flops 4055072 | bytes 2211912 | tf_op jit(solution)/shard_map/rk,kij->rij/dot_general | solution.py:60
  126.4 6.0 %fusion.14 = bf16[2,1024,320]{1,2,0:T(8,128)(2,1)} fusion(f32[40,2,8,1024]{3,2,1,0:T(8,128)} %bitcast.91, f32[320]{0:T(512)S(1)} %copy-done.12, bf16[2,1024,960]{2,1,0:T(8,128)(2,1)} %multiply_convert_fusion, bf16[2,64,960]{2,0,1:T(2,128)(2,1)S(1)} %fusion.17, bf16[2,64,320]{2,0,1:T(2,128)(2,1)S(1)} %convolution_convert_fusion.1), kind=kOutput, calls=%fused_computation.35 | convolution fusion | flops 337641472 | bytes 8193280 | tf_op jit(solution)/shard_map/rpk,rko->rpo/dot_general | solution.py:87
  (72 shorter events, 10.4 us)
Async XLA Ops:
  6.5 1.8 %copy-start = (bf16[16,128,640]{2,1,0:T(8,128)(2,1)S(1)}, bf16[16,128,640]{2,1,0:T(8,128)(2,1)}, u32[]{:S(2)}) copy-start(bf16[16,128,640]{2,1,0:T(8,128)(2,1)} %param.13) | copy-start | bytes 7864324
  10.7 9.0 %copy-start.9 = (bf16[4,64,320]{2,1,0:T(8,128)(2,1)S(1)}, bf16[4,64,320]{2,1,0:T(8,128)(2,1)}, u32[]{:S(2)}) copy-start(bf16[4,64,320]{2,1,0:T(8,128)(2,1)} %param.18) | copy-start | bytes 491524
  14.3 23.8 %copy-start.8 = (bf16[2,1024,320]{1,2,0:T(8,128)(2,1)S(1)}, bf16[2,1024,320]{1,2,0:T(8,128)(2,1)}, u32[]{:S(2)}) copy-start(bf16[2,1024,320]{1,2,0:T(8,128)(2,1)} %param.12) | copy-start | bytes 3932164
  14.3 25.4 %copy-start.16 = (u32[32]{0:T(128)S(1)}, u32[32]{0:T(128)}, u32[]{:S(2)}) copy-start(u32[32]{0:T(128)} %constant.55) | copy-start | bytes 388
  14.3 26.6 %copy-start.15 = (s32[4]{0:T(128)S(1)}, s32[4]{0:T(128)}, u32[]{:S(2)}) copy-start(s32[4]{0:T(128)} %param.16) | copy-start | bytes 52
  14.3 37.7 %all-to-all-start = ((bf16[2,8,128,640]{3,2,0,1:T(8,128)(2,1)}), bf16[2,8,128,640]{3,2,0,1:T(8,128)(2,1)}, u32[]{:S(2)}, u32[]{:S(2)}) async-start(bf16[2,8,128,640]{3,2,0,1:T(8,128)(2,1)} %copy.36), calls=%async_computation | async-start | bytes 5242880 | tf_op jit(solution)/shard_map/all_to_all | solution.py:49
  19.6 31.8 %copy-start.13 = (s32[2]{0:T(128)S(1)}, s32[2]{0:T(128)}, u32[]{:S(2)}) copy-start(s32[2]{0:T(128)} %param.15) | copy-start | bytes 28
  19.6 103.8 %all-gather.2.cloned.1.call-start = ((), (), s32[]{:S(2)}) async-start(), calls=%async_computation.1 | async-start | bytes 2621440 | tf_op jit(solution)/shard_map/all_gather | solution.py:51
  19.8 9.7 %collective-permute-start = (bf16[4,64,320]{2,0,1:T(4,128)(2,1)S(1)}, bf16[4,64,320]{2,0,1:T(4,128)(2,1)S(1)}, u32[]{:S(2)}, u32[]{:S(2)}) collective-permute-start(bf16[4,64,320]{2,0,1:T(4,128)(2,1)S(1)} %copy.48), channel_id=1, source_target_pairs={{0,1},{1,2},{2,3},{3,0},{4,5},{5,6},{6,7},{7,4},{8,9},{9,10},{10,1... | collective-permute-start | bytes 491528 | tf_op jit(solution)/shard_map/ppermute | solution.py:54
  29.6 8.4 %collective-permute-start.1 = (bf16[4,64,320]{2,0,1:T(4,128)(2,1)S(1)}, bf16[4,64,320]{2,0,1:T(4,128)(2,1)S(1)}, u32[]{:S(2)}, u32[]{:S(2)}) collective-permute-start(bf16[4,64,320]{2,0,1:T(4,128)(2,1)S(1)} %collective-permute-done), channel_id=1, source_target_pairs={{0,1},{1,2},{2,3},{3,0},{4,5},{5,6},{6,7},{7,4},{8,9},{9,10},{10,1... | collective-permute-start | bytes 491528 | tf_op jit(solution)/shard_map/ppermute | solution.py:54
  38.0 11.4 %collective-permute-start.2 = (bf16[4,64,320]{2,0,1:T(4,128)(2,1)S(1)}, bf16[4,64,320]{2,0,1:T(4,128)(2,1)S(1)}, u32[]{:S(2)}, u32[]{:S(2)}) collective-permute-start(bf16[4,64,320]{2,0,1:T(4,128)(2,1)S(1)} %collective-permute-done.1), channel_id=1, source_target_pairs={{0,1},{1,2},{2,3},{3,0},{4,5},{5,6},{6,7},{7,4},{8,9},{9,10},{10,1... | collective-permute-start | bytes 491528 | tf_op jit(solution)/shard_map/ppermute | solution.py:54
  54.1 7.8 %copy-start.10 = (f32[960]{0:T(1024)S(1)}, f32[960]{0:T(1024)}, u32[]{:S(2)}) copy-start(f32[960]{0:T(1024)} %param.22) | copy-start | bytes 11524
  54.1 7.8 %copy-start.11 = (f32[960]{0:T(1024)S(1)}, f32[960]{0:T(1024)}, u32[]{:S(2)}) copy-start(f32[960]{0:T(1024)} %param.21) | copy-start | bytes 11524
  61.9 6.9 %copy-start.2 = (bf16[2,1024,320]{2,1,0:T(8,128)(2,1)S(1)}, bf16[2,1024,320]{2,1,0:T(8,128)(2,1)}, u32[]{:S(2)}) copy-start(bf16[2,1024,320]{2,1,0:T(8,128)(2,1)} %copy.53) | copy-start | bytes 3932164
  96.9 4.1 %copy-start.5 = (bf16[2,32,32,960]{3,2,1,0:T(8,128)(2,1)S(1)}, bf16[2,32,32,960]{3,2,1,0:T(8,128)(2,1)}, u32[]{:S(2)}) copy-start(bf16[2,32,32,960]{3,2,1,0:T(8,128)(2,1)} %get-tuple-element.6) | copy-start | bytes 11796484
  96.9 6.9 %slice-start = ((s8[5898240]{0:T(1024)(128)(4,1)}), s8[4194304]{0:T(1024)(128)(4,1)S(1)}, s32[]{:S(2)}) async-start(s8[5898240]{0:T(1024)(128)(4,1)} %bitcast.89), calls=%async_computation.2 | async-start | bytes 8388608
  101.0 2.9 %copy-start.4 = (bf16[2,32,32,960]{3,2,1,0:T(8,128)(2,1)S(1)}, bf16[2,32,32,960]{3,2,1,0:T(8,128)(2,1)}, u32[]{:S(2)}) copy-start(bf16[2,32,32,960]{3,2,1,0:T(8,128)(2,1)} %get-tuple-element.7) | copy-start | bytes 11796484
  101.0 3.0 %slice-start.1 = ((s8[5898240]{0:T(1024)(128)(4,1)}), s8[1703936]{0:T(1024)(128)(4,1)S(1)}, s32[]{:S(2)}) async-start(s8[5898240]{0:T(1024)(128)(4,1)} %bitcast.89), calls=%async_computation.3 | async-start | bytes 3407872
  104.0 2.2 %copy-start.3 = (bf16[2,32,32,960]{3,2,1,0:T(8,128)(2,1)S(1)}, bf16[2,32,32,960]{3,2,1,0:T(8,128)(2,1)}, u32[]{:S(2)}) copy-start(bf16[2,32,32,960]{3,2,1,0:T(8,128)(2,1)} %get-tuple-element.8) | copy-start | bytes 11796484
  106.2 2.2 %copy-start.7 = (bf16[2,32,32,960]{3,2,1,0:T(8,128)(2,1)S(1)}, bf16[2,32,32,960]{3,2,1,0:T(8,128)(2,1)}, u32[]{:S(2)}) copy-start(bf16[2,32,32,960]{3,2,1,0:T(8,128)(2,1)} %get-tuple-element.9) | copy-start | bytes 11796484
  108.4 3.1 %copy-start.6 = (bf16[2,1024,960]{2,1,0:T(8,128)(2,1)S(1)}, bf16[2,1024,960]{2,1,0:T(8,128)(2,1)}, u32[]{:S(2)}) copy-start(bf16[2,1024,960]{2,1,0:T(8,128)(2,1)} %multiply_convert_fusion) | copy-start | bytes 11796484
  118.3 1.9 %copy-start.14 = (bf16[960,320]{0,1:T(8,128)(2,1)S(1)}, bf16[960,320]{0,1:T(8,128)(2,1)}, u32[]{:S(2)}) copy-start(bf16[960,320]{0,1:T(8,128)(2,1)} %param.20) | copy-start | bytes 1843204
  120.2 6.2 %copy-start.12 = (f32[320]{0:T(512)S(1)}, f32[320]{0:T(512)}, u32[]{:S(2)}) copy-start(f32[320]{0:T(512)} %param.23) | copy-start | bytes 3844
  126.4 6.0 %copy-start.1 = (bf16[16,128,640]{2,1,0:T(8,128)(2,1)S(1)}, bf16[16,128,640]{2,1,0:T(8,128)(2,1)}, u32[]{:S(2)}) copy-start(bf16[16,128,640]{2,1,0:T(8,128)(2,1)} %param.13) | copy-start | bytes 7864324
Sparse Core Ops, SparseCore 0:
  38.2 47.3 all-gather.1
